TPU v7x, 128 devices: a whole 4x4x4 slice. The times are simulated.
128 devices in a mesh: row: 8 (over z_lo, x), col: 16 (over z_hi, y, core).
Axes of the slice: x: 4, y: 4, z: 4 (z_hi: 2, z_lo: 2; z = z_hi * 2 + z_lo), core: 2. Of those that a mesh axis runs over, the one named last changes fastest.
Arguments:
- trial: float32 [524288], P(('row', 'col')), may hold values from -6 to 6
- energies: float32 [524288], P(('row', 'col')), may hold values from 0.5 to 3
- densities: bfloat16 [8192, 64, 512], P(('row', 'col')), may hold values from -0.75 to 0.75
- screening: bfloat16 [1048576, 512], P(('row', 'col')), may hold values from 0.0099487305 to 0.099609375
- pair_index: int32 [2, 1048576], P(None, ('row', 'col')), may hold values from 0 to 8191, as said below
- pair_count: int32 [128], P(('row', 'col')), may hold values from 1024 to 8192, as said below
- recycled: float32 [20, 524288], P(None, ('row', 'col'))
Outputs:
- image: float32 [524288], P(('row', 'col'))
- coefficients: float32 [20], replicated
Inputs may be any that keep to these rules, and one draw needn't show every extreme that they name: `pair_index`: slot p of device d = p // 8192 (devices numbered row-major over row and col) holds rows[p] among the k-points of the devices in d's row index and cols[p] among those of the devices in d's col index. `pair_count`: one device is full in every draw.
All inputs are finite; a program needn't handle non-finite values.
Results may differ from a plain program's by a relative error of at most 0.014.
Values may be sent and summed in bfloat16 or wider, within the bound.
No kernel may reach another device: no remote copies, remote signals or barrier semaphores. Data moves between devices by JAX's collectives and lax.ppermute only.
A program may use at most 192 MiB of HBM per device.

v0:
```python
import functools

import jax
import jax.numpy as jnp
import numpy as np
from jax import lax
from jax.experimental import pallas as pl
from jax.experimental.pallas import tpu as pltpu
from jax.sharding import Mesh, PartitionSpec as P

AXES = ("zl", "x", "zh", "y", "c")
F32 = jnp.float32
BF16 = jnp.bfloat16
COPIES = 4
SLOT_MIB = 48
SMALL_MIB = 6
DIAG_FLOPS = 4 * 10**9
STEP = 32
CHUNK = 2048
FIRST = 2048


def slot_kernel(row_index, col_index, count, place, weights, mine, theirs, keep, send,
                rows, cols, sem, part, part_sem, even, odd, rest, *tables):
    fetches = [pltpu.make_async_copy(row_index, rows, sem.at[0]),
               pltpu.make_async_copy(col_index, cols, sem.at[1])]
    for fetch in fetches:
        fetch.start()
    row_tables, col_tables = tables[:COPIES], tables[COPIES:]
    live, core = count[0], place[0]

    def part_copy(i):
        at = pl.ds(pl.multiple_of(i * CHUNK, CHUNK), CHUNK)
        return pltpu.make_async_copy(weights.at[at], part.at[at], part_sem.at[i])

    def part_start(i, _):
        part_copy(i).start()
        return 0

    lax.fori_loop(0, (live + CHUNK - 1) // CHUNK, part_start, 0)
    zeros = jnp.zeros((4, 128), F32)

    half = mine.shape[0] // 2
    block = half // (mine.shape[0] // 512)

    def fill(source, tables, count, dens_first, at):
        def step(i, _):
            part = source[pl.ds(pl.multiple_of(at(i), 16), 16), :].astype(F32)
            for t in range(4):
                dens = part[4 * t:4 * t + 4]
                entry = jnp.concatenate([dens, zeros] if dens_first else [zeros, dens], 0)
                for table in tables:
                    table[pl.ds(pl.multiple_of((i * 4 + t) * 8, 8), 8), :] = entry
            return 0

        lax.fori_loop(0, count // 16, step, 0, unroll=16)

    def whole(i):
        return i * 16

    def one_core(which):
        per = block // 16
        return lambda i: (i // per) * (2 * block) + which * block + (i % per) * 16

    @pl.when(core == 0)
    def _():
        fill(mine, row_tables, 2 * half, True, whole)
        fill(theirs, col_tables, half, False, one_core(0))

    @pl.when(core != 0)
    def _():
        fill(theirs, row_tables, 2 * half, True, whole)
        fill(mine, col_tables, half, False, one_core(1))

    low = lax.broadcasted_iota(jnp.int32, (8, 128), 0) >= 4

    def one(slot, which, row_weight, col_weight):
        r = pl.ds(pl.multiple_of(rows[slot], 8), 8)
        c = pl.ds(pl.multiple_of(cols[slot], 8), 8)
        row_entry = row_tables[which][r, :]
        col_entry = col_tables[which][c, :]
        row_tables[which][r, :] = row_entry + row_weight * col_entry
        col_tables[which][c, :] = col_entry + col_weight * row_entry

    def spread(first, target, at):
        for g in range(STEP // 16):
            v = part[pl.ds(pl.multiple_of(first + g * 16, 16), 16), :].astype(F32)
            for h in range(2):
                for j in range(4):
                    target[pl.ds(at + g * 64 + h * 32 + j * 8, 8), :] = v[8 * h:8 * h + 8, 128 * j:128 * j + 128]

    def many(first, source):
        for g in range(STEP // 16):
            for u in range(8):
                slot = first + g * 16 + u
                both = source[pl.ds(g * 64 + u, 8, stride=8), :]
                turned = jnp.concatenate([both[4:8], both[0:4]], 0)
                one(slot, (2 * u) % COPIES, jnp.where(low, turned, 0.0), jnp.where(low, 0.0, both))
                one(slot + 8, (2 * u + 1) % COPIES, jnp.where(low, both, 0.0), jnp.where(low, 0.0, turned))

    for fetch in fetches:
        fetch.wait()
    pairs = live // (2 * STEP)

    def pair(i, end):
        first = i * (2 * STEP)
        spread(first + STEP, odd, 0)
        many(first, even)
        spread(jnp.minimum(first + 2 * STEP, end * (2 * STEP) - STEP), even, 0)
        many(first + STEP, odd)
        return end

    def phase(n, _):
        begin = n * (FIRST // (2 * STEP))
        end = jnp.where(n == 0, jnp.minimum(pairs, FIRST // (2 * STEP)), pairs)

        def part_wait(i, _):
            part_copy(i).wait()
            return 0

        arrived = jnp.where(n == 0, jnp.minimum(live, FIRST), live)
        lax.fori_loop(n * (FIRST // CHUNK), (arrived + CHUNK - 1) // CHUNK, part_wait, 0)
        spread(begin * (2 * STEP), even, 0)
        lax.fori_loop(begin, end, pair, end)
        return 0

    lax.fori_loop(0, jnp.where(live > FIRST, 2, 1), phase, 0)
    done = pairs * (2 * STEP)
    @pl.when(live > done)
    def _():
        spread(done, rest, 0)
        spread(done + STEP, rest, 4 * STEP)

    def tail(slot, _):
        w = rest[pl.ds(slot // 8 * 32 + slot % 8, 4, stride=8), :]
        w = jnp.concatenate([w, w], 0)
        one(done + slot, 0, jnp.where(low, w, 0.0), jnp.where(low, 0.0, w))
        return 0

    lax.fori_loop(0, live - done, tail, 0)

    def drain(tables, target, count, at, offset):
        def step(i, _):
            parts = []
            for t in range(4):
                entry = pl.ds(pl.multiple_of((i * 4 + t) * 8, 8), 8)
                total = tables[0][entry, :]
                for table in tables[1:]:
                    total = total + table[entry, :]
                parts.append(total[offset:offset + 4])
            rows16 = pl.ds(pl.multiple_of(at(i), 16), 16)
            target[rows16, :] = jnp.concatenate(parts, 0).astype(BF16)
            return 0

        lax.fori_loop(0, count // 16, step, 0, unroll=16)

    def clear(target, at):
        def step(i, _):
            target[pl.ds(pl.multiple_of(at(i), 16), 16), :] = jnp.zeros((16, 128), BF16)
            return 0

        lax.fori_loop(0, half // 16, step, 0, unroll=8)

    @pl.when(core == 0)
    def _():
        drain(row_tables, keep, 2 * half, whole, 4)
        drain(col_tables, send, half, one_core(0), 0)
        clear(send, one_core(1))

    @pl.when(core != 0)
    def _():
        drain(row_tables, send, 2 * half, whole, 4)
        drain(col_tables, keep, half, one_core(1), 0)
        clear(keep, one_core(0))


def pair_terms(rows, cols, count, place, weights, mine, theirs):
    smem = pl.BlockSpec(memory_space=pltpu.SMEM)
    vmem = pl.BlockSpec(memory_space=pltpu.VMEM)
    hold = pl.BlockSpec(memory_space=pl.ANY)
    row_table = pltpu.VMEM((2 * mine.shape[0], 128), F32)
    col_table = pltpu.VMEM((mine.shape[0], 128), F32)
    return pl.pallas_call(
        slot_kernel,
        out_shape=[jax.ShapeDtypeStruct(mine.shape, BF16)] * 2,
        in_specs=[hold] * 2 + [smem] * 2 + [hold, vmem, vmem],
        out_specs=[vmem, vmem],
        scratch_shapes=[
            *[pltpu.SMEM(rows.shape, jnp.int32)] * 2, pltpu.SemaphoreType.DMA((2,)),
            pltpu.VMEM(weights.shape, BF16), pltpu.SemaphoreType.DMA((weights.shape[0] // CHUNK,)),
            *[pltpu.VMEM((STEP * 4, 128), F32)] * 2, pltpu.VMEM((STEP * 8, 128), F32),
            *[row_table] * COPIES, *[col_table] * COPIES],
        compiler_params=pltpu.CompilerParams(vmem_limit_bytes=SLOT_MIB * 2**20),
    )(rows, cols, count, place, weights, mine, theirs)


def local_call(kernel, outs, *args, scalars=0, flops=0):
    smem = pl.BlockSpec(memory_space=pltpu.SMEM)
    vmem = pl.BlockSpec(memory_space=pltpu.VMEM)
    return pl.pallas_call(
        kernel,
        out_shape=outs,
        in_specs=[smem] * scalars + [vmem] * (len(args) - scalars),
        out_specs=jax.tree.map(lambda _: vmem, outs),
        cost_estimate=pl.CostEstimate(flops=flops, bytes_accessed=0, transcendentals=0) if flops else None,
        compiler_params=pltpu.CompilerParams(vmem_limit_bytes=SMALL_MIB * 2**20),
    )(*args)


def pack_kernel(kpoints, spans, place, first_row, local, other, pair_index, out, rows, cols):
    index = pair_index[...]
    rows[...] = ((index[0:1, :] - first_row[0]) * 8).reshape(rows.shape)
    col = index[1:2, :]
    cols[...] = ((col // spans * kpoints + col % kpoints) * 8).reshape(cols.shape)
    size = local.shape[0]

    def step(i, _):
        at = pl.ds(pl.multiple_of(i * 16, 16), 16)
        first, second = local[at, :], other[at, :]
        swapped = place[0] != 0
        low = jnp.where(swapped, second.astype(F32), first.astype(F32)).astype(BF16)
        high = jnp.where(swapped, first.astype(F32), second.astype(F32)).astype(BF16)
        for n in range(out.shape[0]):
            out[n, at, :] = low
            out[n, pl.ds(pl.multiple_of(size + i * 16, 16), 16), :] = high
        return 0

    lax.fori_loop(0, size // 16, step, 0, unroll=2)


def add_kernel(keep, got, out):
    def step(i, _):
        at = pl.ds(pl.multiple_of(i * 16, 16), 16)
        out[at, :] = (keep[at, :].astype(F32) + got[at, :].astype(F32)).astype(BF16)
        return 0

    lax.fori_loop(0, keep.shape[0] // 16, step, 0, unroll=8)


def sum_kernel(place, parts, here, there):
    size = here.shape[0]

    def step(i, _):
        at = pl.ds(pl.multiple_of(i * 16, 16), 16)
        for target, which in ((here, place[0]), (there, 1 - place[0])):
            first = pl.ds(pl.multiple_of(which * size + i * 16, 16), 16)
            total = parts[0, first, :].astype(F32)
            for n in range(1, parts.shape[0]):
                total = total + parts[n, first, :].astype(F32)
            target[at, :] = total
        return 0

    lax.fori_loop(0, size // 16, step, 0, unroll=4)


def diagonal_kernel(trial, out):
    span = out.shape[1]
    rows8 = lax.broadcasted_iota(jnp.int32, (8, span), 0)
    owner = lax.broadcasted_iota(jnp.int32, (8, span), 1) // (span // 8)
    for g in range(out.shape[0] // 16):
        both = []
        for n in (2 * g, 2 * g + 1):
            line = jnp.broadcast_to(trial[n * span:(n + 1) * span].reshape(1, span), (8, span))
            both.append(jnp.where(rows8 == owner, line, 0.0))
        out[16 * g:16 * g + 16, :] = jnp.concatenate(both, 0).astype(BF16)


def project_kernel(diagonal, densities, out, wide):
    kpoints, span = diagonal.shape
    for g in range(kpoints // 16):
        pair = diagonal[16 * g:16 * g + 16, :]
        for h in range(2):
            n = 2 * g + h
            dens = jnp.dot(pair[8 * h:8 * h + 8, :], densities[n * span:(n + 1) * span, :], preferred_element_type=F32)
            for j in range(4):
                wide[pl.ds(32 * n + j, 8, stride=4), :] = dens[:, 128 * j:128 * j + 128]
    out[...] = wide[...].astype(BF16)


def project(trial, densities):
    kpoints, transitions, gvectors = densities.shape
    vmem = pl.BlockSpec(memory_space=pltpu.VMEM)
    diagonal = local_call(
        diagonal_kernel, jax.ShapeDtypeStruct((kpoints, 8 * transitions), BF16), trial, flops=DIAG_FLOPS)
    return pl.pallas_call(
        project_kernel,
        out_shape=jax.ShapeDtypeStruct((kpoints * 4, 128), BF16),
        in_specs=[vmem, vmem],
        out_specs=vmem,
        scratch_shapes=[pltpu.VMEM((kpoints * 4, 128), F32)],
        cost_estimate=pl.CostEstimate(flops=4 * 10**9, bytes_accessed=0, transcendentals=0),
        compiler_params=pltpu.CompilerParams(vmem_limit_bytes=SMALL_MIB * 2**20),
    )(diagonal, densities.reshape(-1, gvectors))


def expand_kernel(here, there, densities, trial, energies, recycled, product, projections):
    kpoints = here.shape[0] // 4
    span = densities.shape[0] * 8 // kpoints
    rows8 = lax.broadcasted_iota(jnp.int32, (8, span), 0)
    owner = lax.broadcasted_iota(jnp.int32, (8, span), 1) // (span // 8)
    sums = jnp.zeros((recycled.shape[0], 128), F32)
    for g in range(kpoints // 8):
        field = []
        for j in range(4):
            at = pl.ds(32 * g + j, 8, stride=4)
            field.append(here[at, :] + there[at, :])
        every = lax.dot_general(
            jnp.concatenate(field, 1).astype(BF16), densities[g * span:(g + 1) * span, :],
            (((1,), (1,)), ((), ())), preferred_element_type=F32)
        part = jnp.sum(jnp.where(rows8 == owner, every, 0.0), 0, keepdims=True)
        at = pl.ds(g * span, span)
        line = (energies[at] * trial[at]).reshape(1, span) + part
        product[at] = line.reshape(span)
        weighted = recycled[:, g * span:(g + 1) * span] * line
        for j in range(span // 128):
            sums = sums + weighted[:, 128 * j:128 * j + 128]
    total = jnp.sum(sums, 1, keepdims=True)
    count = total.shape[0]
    at = lax.broadcasted_iota(jnp.int32, (count, 128), 0) == lax.broadcasted_iota(jnp.int32, (count, 128), 1)
    line = jnp.sum(jnp.where(at, total, 0.0), 0, keepdims=True)
    projections[...] = jnp.broadcast_to(line, projections.shape)


def expand(here, there, densities, trial, energies, recycled, devices):
    gvectors = densities.shape[-1]
    vmem = pl.BlockSpec(memory_space=pltpu.VMEM)
    return pl.pallas_call(
        expand_kernel,
        out_shape=[jax.ShapeDtypeStruct(trial.shape, F32), jax.ShapeDtypeStruct((devices, 128), F32)],
        in_specs=[vmem] * 6,
        out_specs=[vmem] * 2,
        compiler_params=pltpu.CompilerParams(vmem_limit_bytes=SMALL_MIB * 2**20),
    )(here, there, densities.reshape(-1, gvectors), trial, energies, recycled)


def finish_kernel(product, recycled, arrived, image, coefficients):
    line = jnp.sum(arrived[...], 0, keepdims=True)
    count = recycled.shape[0]
    coefficients[...] = line[:, :count].reshape(count)
    at = lax.broadcasted_iota(jnp.int32, (count, 128), 0) == lax.broadcasted_iota(jnp.int32, (count, 128), 1)
    column = jnp.sum(jnp.where(at, jnp.broadcast_to(line, (count, 128)), 0.0), 1, keepdims=True)
    span = 512
    for g in range(product.shape[0] // span):
        taken = jnp.sum(recycled[:, g * span:(g + 1) * span] * column, 0, keepdims=True)
        at = pl.ds(g * span, span)
        image[at] = product[at] - taken.reshape(span)


def finish(product, recycled, arrived):
    vmem = pl.BlockSpec(memory_space=pltpu.VMEM)
    return pl.pallas_call(
        finish_kernel,
        out_shape=[jax.ShapeDtypeStruct(product.shape, F32), jax.ShapeDtypeStruct(recycled.shape[:1], F32)],
        in_specs=[vmem] * 3,
        out_specs=[vmem] * 2,
        compiler_params=pltpu.CompilerParams(vmem_limit_bytes=SMALL_MIB * 2**20),
    )(product, recycled, arrived)


def chip_groups(along_row, along_col):
    ids = np.arange(along_row * along_col * 2).reshape(along_row, along_col, 2)
    return [g.tolist() for g in ids[:, :, 0]] + [g.tolist() for g in ids[:, :, 1].T]


def body(trial, energies, densities, screening, pair_index, pair_count, recycled):
    kpoints, transitions, gvectors = densities.shape
    lanes = 128
    per_k = gvectors // lanes
    row_chips = lax.axis_size("zl") * lax.axis_size("x")
    col_chips = lax.axis_size("zh") * lax.axis_size("y")
    cores = lax.axis_size("c")
    col_devices = col_chips * cores
    row_place = lax.axis_index("zl") * lax.axis_size("x") + lax.axis_index("x")
    core = lax.axis_index("c")
    swap = [(0, 1), (1, 0)]
    groups = chip_groups(row_chips, col_chips)

    first_row = jnp.reshape(row_place * col_devices * kpoints, (1,)).astype(jnp.int32)
    local_dens = project(trial, densities)
    from_other = lax.ppermute(local_dens, "c", swap)
    place = core.reshape(1).astype(jnp.int32)
    out = jax.ShapeDtypeStruct((row_chips, 2 * local_dens.shape[0], lanes), BF16)
    index = jax.ShapeDtypeStruct(pair_index.shape[1:], jnp.int32)
    spread, rows, cols = local_call(
        functools.partial(pack_kernel, kpoints, col_devices * kpoints), [out, index, index],
        place, first_row, local_dens, from_other, pair_index, scalars=2)
    mine = lax.all_to_all(spread, AXES, 0, 0, axis_index_groups=groups).reshape(-1, lanes)
    theirs = lax.ppermute(mine, "c", swap)

    keep, send = pair_terms(rows, cols, pair_count, place, screening, mine, theirs)

    got = lax.ppermute(send, "c", swap)
    total = local_call(add_kernel, jax.ShapeDtypeStruct(keep.shape, BF16), keep, got)
    parts = lax.all_to_all(
        total.reshape(row_chips, -1, lanes), AXES, 0, 0, axis_index_groups=groups)
    part = jax.ShapeDtypeStruct((kpoints * per_k, lanes), F32)
    here, there = local_call(sum_kernel, [part, part], place, parts, scalars=1)
    devices = row_chips * col_devices
    product, projections = expand(
        here, lax.ppermute(there, "c", swap), densities, trial, energies, recycled, devices)
    arrived = lax.all_to_all(projections, AXES, 0, 0, tiled=True)
    return tuple(finish(product, recycled, arrived))


def solution(mesh):
    fine = Mesh(mesh.devices.reshape(2, 4, 2, 4, 2), AXES)
    placed = (
        P(AXES),
        P(AXES),
        P(AXES, None, None),
        P(AXES, None),
        P(None, AXES),
        P(AXES),
        P(None, AXES),
    )
    return jax.shard_map(
        body, mesh=fine, in_specs=placed, out_specs=(P(AXES), P()), check_vma=False
    )
```

profile of v0, /device:TPU:1, one launch (start us, length us, event | category | flops | bytes accessed | tf_op | source)
XLA Modules:
  0.0 87.1 jit_solution(3179476351317413853)
XLA Ops:
  0.6 0.0 copy-start
  0.6 0.0 copy-start.4
  0.7 0.9 copy-done.4
  1.5 0.0 copy-start.3
  1.5 1.3 %copy-done = bf16[64,64,512]{2,1,0:T(8,128)(2,1)S(1)} copy-done((bf16[64,64,512]{2,1,0:T(8,128)(2,1)S(1)}, bf16[64,64,512]{2,1,0:T(8,128)(2,1)}, u32[]{:S(2)}) %copy-start) | copy-done | bytes 4194328
  2.8 0.7 shard_map.87.local
  3.5 1.4 %collective-permute-start = (bf16[256,128]{1,0:T(8,128)(2,1)S(1)}, bf16[256,128]{1,0:T(8,128)(2,1)S(1)}, u32[]{:S(2)}, u32[]{:S(2)}) collective-permute-start(bf16[256,128]{1,0:T(8,128)(2,1)S(1)} %shard_map.87.local), channel_id=1, source_target_pairs={{0,1},{1,0},{2,3},{3,2},{4,5},{5,4},{6,7},{7,6},{8,9},{9,8},{10,11... | collective-permute-start | bytes 196616 | tf_op jit(solution)/shard_map/ppermute | solution.py:380
  4.9 0.9 %collective-permute-done.other = bf16[256,128]{1,0:T(8,128)(2,1)S(1)} collective-permute-done((bf16[256,128]{1,0:T(8,128)(2,1)S(1)}, bf16[256,128]{1,0:T(8,128)(2,1)S(1)}, u32[]{:S(2)}, u32[]{:S(2)}) %collective-permute-start) | collective-permute-done | bytes 65568 | tf_op jit(solution)/shard_map/ppermute | solution.py:380
  5.8 0.0 copy-done.3
  5.8 0.3 shard_map.88
  6.1 17.2 %all_to_all.21 = bf16[8,512,128]{2,1,0:T(8,128)(2,1)S(1)} all-to-all(bf16[8,512,128]{2,1,0:T(8,128)(2,1)S(1)} %get-tuple-element.13), channel_id=1, replica_groups={{0,2,4,6,8,10,12,14},{16,18,20,22,24,26,28,30},{32,34,36,38,40,42,44,46..., dimensions={0} | all-to-all | bytes 2097152 | tf_op jit(solution)/shard_map/all_to_all | solution.py:387
  23.3 5.6 %collective-permute-start.1 = (bf16[4096,128]{1,0:T(8,128)(2,1)S(1)}, bf16[4096,128]{1,0:T(8,128)(2,1)S(1)}, u32[]{:S(2)}, u32[]{:S(2)}) collective-permute-start(bf16[4096,128]{1,0:T(8,128)(2,1)S(1)} %bitcast.12), channel_id=1, source_target_pairs={{0,1},{1,0},{2,3},{3,2},{4,5},{5,4},{6,7},{7,6},{8,9},{9,8},{10,11... | collective-permute-start | bytes 3145736 | tf_op jit(solution)/shard_map/ppermute | solution.py:388
  29.5 1.6 %collective-permute-done.1.theirs = bf16[4096,128]{1,0:T(8,128)(2,1)S(1)} collective-permute-done((bf16[4096,128]{1,0:T(8,128)(2,1)S(1)}, bf16[4096,128]{1,0:T(8,128)(2,1)S(1)}, u32[]{:S(2)}, u32[]{:S(2)}) %collective-permute-start.1) | collective-permute-done | bytes 1048608 | tf_op jit(solution)/shard_map/ppermute | solution.py:388
  31.1 0.0 copy-start.1
  31.1 0.0 copy-start.2
  31.1 0.0 copy-start.5
  31.1 0.0 copy-start.6
  31.1 12.4 %shard_map.89 = (bf16[4096,128]{1,0:T(8,128)(2,1)S(1)}, bf16[4096,128]{1,0:T(8,128)(2,1)S(1)}) custom-call(s32[8192]{0:T(1024)S(1)} %get-tuple-element.11.row_index, s32[8192]{0:T(1024)S(1)} %get-tuple-element.12.col_index, s32[1]{0:T(128)S(6)} %copy.10.count, s32[1]{0:T(128)} %bitcast.place, bf16[8192,512]{1,0:T(8,128)(2,1)} %weights.1, ...), custom_call_target="tpu_custom_call" | custom-call | tf_op jit(solution)/shard_map/pallas_call | solution.py:183
  43.5 0.7 collective-permute-start.2
  44.2 2.3 %collective-permute-done.2.got = bf16[4096,128]{1,0:T(8,128)(2,1)S(1)} collective-permute-done((bf16[4096,128]{1,0:T(8,128)(2,1)S(1)}, bf16[4096,128]{1,0:T(8,128)(2,1)S(1)}, u32[]{:S(2)}, u32[]{:S(2)}) %collective-permute-start.2) | collective-permute-done | bytes 1048608 | tf_op jit(solution)/shard_map/ppermute | solution.py:392
  46.5 0.5 shard_map.90
  47.0 20.0 %all_to_all.22.parts = bf16[8,512,128]{2,1,0:T(8,128)(2,1)S(1)} all-to-all(bf16[8,512,128]{2,1,0:T(8,128)(2,1)S(1)} %bitcast.9), channel_id=1, replica_groups={{0,2,4,6,8,10,12,14},{16,18,20,22,24,26,28,30},{32,34,36,38,40,42,44,46..., dimensions={0} | all-to-all | bytes 2097152 | tf_op jit(solution)/shard_map/all_to_all | solution.py:394
  67.0 0.2 shard_map.91
  67.2 0.1 collective-permute-start.3
  67.3 1.3 %collective-permute-done.3.there = f32[256,128]{1,0:T(8,128)S(1)} collective-permute-done((f32[256,128]{1,0:T(8,128)S(1)}, f32[256,128]{1,0:T(8,128)S(1)}, u32[]{:S(2)}, u32[]{:S(2)}) %collective-permute-start.3) | collective-permute-done | bytes 131104 | tf_op jit(solution)/shard_map/ppermute | solution.py:400
  68.6 0.0 copy-done.1
  68.6 0.0 copy-done.2
  68.6 0.0 copy-done.5
  68.6 0.0 copy-done.6
  68.6 1.3 %shard_map.92 = (f32[4096]{0:T(1024)S(1)}, f32[128,128]{1,0:T(8,128)S(1)}) custom-call(f32[256,128]{1,0:T(8,128)S(1)} %get-tuple-element.16.here, f32[256,128]{1,0:T(8,128)S(1)} %collective-permute-done.3.there, bf16[4096,512]{1,0:T(8,128)(2,1)S(1)} %bitcast.11, f32[4096]{0:T(1024)S(1)} %copy-done.5, f32[4096]{0:T(1024)S(1)} %copy-done.6, ...), custom_call_target="tpu_custom_call" | custom-call | tf_op jit(solution)/shard_map/pallas_call | solution.py:327
  70.0 16.3 %all_to_all.23 = f32[128,1,128]{2,1,0:T(1,128)S(1)} all-to-all(f32[128,1,128]{2,1,0:T(1,128)S(1)} %bitcast.15), channel_id=1, replica_groups=mesh['zl'=2,'x'=4,'zh'=2,'y'=4,'c'=2] {'zl','x','zh','y','c'}, dimensions={0} | all-to-all | bytes 131072 | tf_op jit(solution)/shard_map/all_to_all | solution.py:401
  86.3 0.8 shard_map.93
  (1 shorter events, 0.0 us)
Async XLA Ops:
  0.6 2.2 %copy-start = (bf16[64,64,512]{2,1,0:T(8,128)(2,1)S(1)}, bf16[64,64,512]{2,1,0:T(8,128)(2,1)}, u32[]{:S(2)}) copy-start(bf16[64,64,512]{2,1,0:T(8,128)(2,1)} %param.9) | copy-start | bytes 12582916
  0.6 0.9 copy-start.4
  1.5 4.3 %copy-start.3 = (s32[2,8192]{1,0:T(2,128)S(1)}, s32[2,8192]{1,0:T(2,128)}, u32[]{:S(2)}) copy-start(s32[2,8192]{1,0:T(2,128)} %pair_index.1) | copy-start | bytes 196612
  3.5 2.3 %collective-permute-start = (bf16[256,128]{1,0:T(8,128)(2,1)S(1)}, bf16[256,128]{1,0:T(8,128)(2,1)S(1)}, u32[]{:S(2)}, u32[]{:S(2)}) collective-permute-start(bf16[256,128]{1,0:T(8,128)(2,1)S(1)} %shard_map.87.local), channel_id=1, source_target_pairs={{0,1},{1,0},{2,3},{3,2},{4,5},{5,4},{6,7},{7,6},{8,9},{9,8},{10,11... | collective-permute-start | bytes 196616 | tf_op jit(solution)/shard_map/ppermute | solution.py:380
  23.3 7.8 %collective-permute-start.1 = (bf16[4096,128]{1,0:T(8,128)(2,1)S(1)}, bf16[4096,128]{1,0:T(8,128)(2,1)S(1)}, u32[]{:S(2)}, u32[]{:S(2)}) collective-permute-start(bf16[4096,128]{1,0:T(8,128)(2,1)S(1)} %bitcast.12), channel_id=1, source_target_pairs={{0,1},{1,0},{2,3},{3,2},{4,5},{5,4},{6,7},{7,6},{8,9},{9,8},{10,11... | collective-permute-start | bytes 3145736 | tf_op jit(solution)/shard_map/ppermute | solution.py:388
  31.1 37.5 %copy-start.1 = (bf16[64,64,512]{2,1,0:T(8,128)(2,1)S(1)}, bf16[64,64,512]{2,1,0:T(8,128)(2,1)}, u32[]{:S(2)}) copy-start(bf16[64,64,512]{2,1,0:T(8,128)(2,1)} %param.9) | copy-start | bytes 12582916
  31.1 37.5 %copy-start.2 = (f32[20,4096]{1,0:T(8,128)S(1)}, f32[20,4096]{1,0:T(8,128)}, u32[]{:S(2)}) copy-start(f32[20,4096]{1,0:T(8,128)} %recycled.3) | copy-start | bytes 983044
  31.1 37.5 %copy-start.5 = (f32[4096]{0:T(1024)S(1)}, f32[4096]{0:T(1024)}, u32[]{:S(2)}) copy-start(f32[4096]{0:T(1024)} %trial.3) | copy-start | bytes 49156
  31.1 37.5 %copy-start.6 = (f32[4096]{0:T(1024)S(1)}, f32[4096]{0:T(1024)}, u32[]{:S(2)}) copy-start(f32[4096]{0:T(1024)} %energies.1) | copy-start | bytes 49156
  43.5 2.9 %collective-permute-start.2 = (bf16[4096,128]{1,0:T(8,128)(2,1)S(1)}, bf16[4096,128]{1,0:T(8,128)(2,1)S(1)}, u32[]{:S(2)}, u32[]{:S(2)}) collective-permute-start(bf16[4096,128]{1,0:T(8,128)(2,1)S(1)} %get-tuple-element.15), channel_id=1, source_target_pairs={{0,1},{1,0},{2,3},{3,2},{4,5},{5,4},{6,7},{7,6},{8,9},{9,8},{10,11... | collective-permute-start | bytes 3145736 | tf_op jit(solution)/shard_map/ppermute | solution.py:392
  67.2 1.4 %collective-permute-start.3 = (f32[256,128]{1,0:T(8,128)S(1)}, f32[256,128]{1,0:T(8,128)S(1)}, u32[]{:S(2)}, u32[]{:S(2)}) collective-permute-start(f32[256,128]{1,0:T(8,128)S(1)} %get-tuple-element.17), channel_id=1, source_target_pairs={{0,1},{1,0},{2,3},{3,2},{4,5},{5,4},{6,7},{7,6},{8,9},{9,8},{10,11... | collective-permute-start | bytes 393224 | tf_op jit(solution)/shard_map/ppermute | solution.py:400
where the time goes:
time: 87.8 us; the launch traced here: 87.1 us
  blocking collectives  53.5 us (61%)
  Pallas kernels  16.1 us (18%)
  starting transfers between devices  7.74 us (9%)
  waiting for transfers between devices  6.16 us (7%)
  local copies, waits for them, and re-layouts  2.18 us (2%)
  between operations  1.37 us (2%)
    all_to_all x1, blocking collectives, body(): lax.all_to_all(total.reshape(row_chips, -1, lanes), AXES, 0, 0, axis_inde...  20 us
    all_to_all x1, blocking collectives, body(): lax.all_to_all(spread, AXES, 0, 0, axis_index_groups=groups)  17.2 us
    all_to_all x1, blocking collectives, body(): arrived = lax.all_to_all(projections, AXES, 0, 0, tiled=True)  16.3 us
    pallas_call x1, Pallas kernels, pair_terms(): pl.pallas_call(slot_kernel, out_shape=[jax.ShapeDtypeStruct(mine.shape, B...  12.4 us
    ppermute x1, starting transfers between devices, body(): theirs = lax.ppermute(mine, 'c', swap)  5.56 us
    ppermute x1, waiting for transfers between devices, body(): got = lax.ppermute(send, 'c', swap)  2.29 us
    unnamed x14, local copies, waits for them, and re-layouts  2.18 us
  transfers between devices with their start and end apart: 4, of which 4 were waited for; matrix products, arithmetic and copies ran while one was open for 0% of the time, Pallas kernels for 0%

commit v1 on v0

--- a/solution.py
+++ b/solution.py
@@ -237,17 +237,15 @@
     lax.fori_loop(0, keep.shape[0] // 16, step, 0, unroll=8)
 
 
-def sum_kernel(place, parts, here, there):
-    size = here.shape[0]
+def sum_kernel(which, parts, out):
+    size = out.shape[0]
 
     def step(i, _):
-        at = pl.ds(pl.multiple_of(i * 16, 16), 16)
-        for target, which in ((here, place[0]), (there, 1 - place[0])):
-            first = pl.ds(pl.multiple_of(which * size + i * 16, 16), 16)
-            total = parts[0, first, :].astype(F32)
-            for n in range(1, parts.shape[0]):
-                total = total + parts[n, first, :].astype(F32)
-            target[at, :] = total
+        first = pl.ds(pl.multiple_of(which[0] * size + i * 16, 16), 16)
+        total = parts[0, first, :].astype(F32)
+        for n in range(1, parts.shape[0]):
+            total = total + parts[n, first, :].astype(F32)
+        out[pl.ds(pl.multiple_of(i * 16, 16), 16), :] = total.astype(out.dtype)
         return 0
 
     lax.fori_loop(0, size // 16, step, 0, unroll=4)
@@ -293,17 +291,18 @@
     )(diagonal, densities.reshape(-1, gvectors))
 
 
-def expand_kernel(here, there, densities, trial, energies, recycled, product, projections):
+def expand_kernel(here, there, densities, trial, energies, recycled, product, projections, field_sum):
     kpoints = here.shape[0] // 4
     span = densities.shape[0] * 8 // kpoints
     rows8 = lax.broadcasted_iota(jnp.int32, (8, span), 0)
     owner = lax.broadcasted_iota(jnp.int32, (8, span), 1) // (span // 8)
     sums = jnp.zeros((recycled.shape[0], 128), F32)
+    field_sum[...] = here[...] + there[...].astype(F32)
     for g in range(kpoints // 8):
         field = []
         for j in range(4):
             at = pl.ds(32 * g + j, 8, stride=4)
-            field.append(here[at, :] + there[at, :])
+            field.append(field_sum[at, :])
         every = lax.dot_general(
             jnp.concatenate(field, 1).astype(BF16), densities[g * span:(g + 1) * span, :],
             (((1,), (1,)), ((), ())), preferred_element_type=F32)
@@ -329,6 +328,7 @@
         out_shape=[jax.ShapeDtypeStruct(trial.shape, F32), jax.ShapeDtypeStruct((devices, 128), F32)],
         in_specs=[vmem] * 6,
         out_specs=[vmem] * 2,
+        scratch_shapes=[pltpu.VMEM(here.shape, F32)],
         compiler_params=pltpu.CompilerParams(vmem_limit_bytes=SMALL_MIB * 2**20),
     )(here, there, densities.reshape(-1, gvectors), trial, energies, recycled)
 
@@ -393,8 +393,10 @@
     total = local_call(add_kernel, jax.ShapeDtypeStruct(keep.shape, BF16), keep, got)
     parts = lax.all_to_all(
         total.reshape(row_chips, -1, lanes), AXES, 0, 0, axis_index_groups=groups)
-    part = jax.ShapeDtypeStruct((kpoints * per_k, lanes), F32)
-    here, there = local_call(sum_kernel, [part, part], place, parts, scalars=1)
+    part = (kpoints * per_k, lanes)
+    away = (1 - core).reshape(1).astype(jnp.int32)
+    there = local_call(sum_kernel, jax.ShapeDtypeStruct(part, BF16), away, parts, scalars=1)
+    here = local_call(sum_kernel, jax.ShapeDtypeStruct(part, F32), place, parts, scalars=1)
     devices = row_chips * col_devices
     product, projections = expand(
         here, lax.ppermute(there, "c", swap), densities, trial, energies, recycled, devices)

time: 87.8 us -> 91.7 us (1.044)
  blocking collectives: 53.5 us -> 36 us
  starting transfers between devices: 7.74 us -> 19.6 us
  waiting for transfers between devices: 6.16 us -> 16.6 us
  Pallas kernels: 16.1 us -> 13.7 us
  local copies, waits for them, and re-layouts: 2.18 us -> 4.36 us
    all_to_all x1 -> x0, blocking collectives: 20 us -> none  [body(): lax.all_to_all(total.reshape(row_chips, -1, lanes), AXES, 0, 0, axis_inde...]
    all_to_all x0 -> x1, waiting for transfers between devices: none -> 10.6 us  [body(): lax.all_to_all(total.reshape(row_chips, -1, lanes), AXES, 0, 0, axis_inde...]
    all_to_all x0 -> x1, starting transfers between devices: none -> 8.78 us  [body(): lax.all_to_all(total.reshape(row_chips, -1, lanes), AXES, 0, 0, axis_inde...]
    ppermute x1, starting transfers between devices: 0.09 us -> 3.69 us  [body(): lax.ppermute(there, 'c', swap)]
    pallas_call x1, Pallas kernels: 12.4 us -> 8.89 us  [pair_terms(): pl.pallas_call(slot_kernel, out_shape=[jax.ShapeDtypeStruct(mine.shape, B...]
    all_to_all x1, blocking collectives: 16.3 us -> 18.8 us  [body(): arrived = lax.all_to_all(projections, AXES, 0, 0, tiled=True)]
    unnamed x14, local copies, waits for them, and re-layouts: 2.18 us -> 4.36 us
    pallas_call x4 -> x5, Pallas kernels: 1 us -> 2.04 us  [local_call(): pl.pallas_call(kernel, out_shape=outs, in_specs=[smem] * scalars + [vmem]...]
  transfers between devices with their start and end apart: 4 -> 5, of which waited for: 4 -> 5; matrix products, arithmetic and copies ran while one was open for 0% -> 0% of each run, Pallas kernels for 0% -> 0%
where the time goes in v1:
time: 91.7 us; the launch traced here: 91.6 us
  blocking collectives  36 us (39%)
  starting transfers between devices  19.6 us (21%)
  waiting for transfers between devices  16.6 us (18%)
  Pallas kernels  13.7 us (15%)
  local copies, waits for them, and re-layouts  4.36 us (5%)
  between operations  1.37 us (1%)
    all_to_all x1, blocking collectives, body(): arrived = lax.all_to_all(projections, AXES, 0, 0, tiled=True)  18.8 us
    all_to_all x1, blocking collectives, body(): lax.all_to_all(spread, AXES, 0, 0, axis_index_groups=groups)  17.2 us
    all_to_all x1, waiting for transfers between devices, body(): lax.all_to_all(total.reshape(row_chips, -1, lanes), AXES, 0, 0, axis_inde...  10.6 us
    pallas_call x1, Pallas kernels, pair_terms(): pl.pallas_call(slot_kernel, out_shape=[jax.ShapeDtypeStruct(mine.shape, B...  8.89 us
    all_to_all x1, starting transfers between devices, body(): lax.all_to_all(total.reshape(row_chips, -1, lanes), AXES, 0, 0, axis_inde...  8.78 us
    ppermute x1, starting transfers between devices, body(): theirs = lax.ppermute(mine, 'c', swap)  5.56 us
    unnamed x14, local copies, waits for them, and re-layouts  4.36 us
    ppermute x1, starting transfers between devices, body(): lax.ppermute(there, 'c', swap)  3.69 us
  transfers between devices with their start and end apart: 5, of which 5 were waited for; matrix products, arithmetic and copies ran while one was open for 0% of the time, Pallas kernels for 0%

profile of v1, /device:TPU:1, one launch (start us, length us, event | category | flops | bytes accessed | tf_op | source)
XLA Modules:
  0.0 91.6 jit_solution(12339670419209135807)
XLA Ops:
  0.6 0.0 copy-start
  0.6 0.0 copy-start.4
  0.7 0.9 copy-done.4
  1.5 0.0 copy-start.3
  1.5 1.3 %copy-done = bf16[64,64,512]{2,1,0:T(8,128)(2,1)S(1)} copy-done((bf16[64,64,512]{2,1,0:T(8,128)(2,1)S(1)}, bf16[64,64,512]{2,1,0:T(8,128)(2,1)}, u32[]{:S(2)}) %copy-start) | copy-done | bytes 4194328
  2.8 0.7 shard_map.87.local
  3.5 1.4 %collective-permute-start = (bf16[256,128]{1,0:T(8,128)(2,1)S(1)}, bf16[256,128]{1,0:T(8,128)(2,1)S(1)}, u32[]{:S(2)}, u32[]{:S(2)}) collective-permute-start(bf16[256,128]{1,0:T(8,128)(2,1)S(1)} %shard_map.87.local), channel_id=1, source_target_pairs={{0,1},{1,0},{2,3},{3,2},{4,5},{5,4},{6,7},{7,6},{8,9},{9,8},{10,11... | collective-permute-start | bytes 196616 | tf_op jit(solution)/shard_map/ppermute | solution.py:380
  4.9 0.9 collective-permute-done.other
  5.8 0.0 copy-done.3
  5.8 0.3 shard_map.88
  6.1 17.2 %all_to_all.21 = bf16[8,512,128]{2,1,0:T(8,128)(2,1)S(1)} all-to-all(bf16[8,512,128]{2,1,0:T(8,128)(2,1)S(1)} %get-tuple-element.11), channel_id=1, replica_groups={{0,2,4,6,8,10,12,14},{16,18,20,22,24,26,28,30},{32,34,36,38,40,42,44,46..., dimensions={0} | all-to-all | bytes 2097152 | tf_op jit(solution)/shard_map/all_to_all | solution.py:387
  23.3 5.6 %collective-permute-start.1 = (bf16[4096,128]{1,0:T(8,128)(2,1)S(1)}, bf16[4096,128]{1,0:T(8,128)(2,1)S(1)}, u32[]{:S(2)}, u32[]{:S(2)}) collective-permute-start(bf16[4096,128]{1,0:T(8,128)(2,1)S(1)} %bitcast.12), channel_id=1, source_target_pairs={{0,1},{1,0},{2,3},{3,2},{4,5},{5,4},{6,7},{7,6},{8,9},{9,8},{10,11... | collective-permute-start | bytes 3145736 | tf_op jit(solution)/shard_map/ppermute | solution.py:388
  29.5 1.6 %collective-permute-done.1.theirs = bf16[4096,128]{1,0:T(8,128)(2,1)S(1)} collective-permute-done((bf16[4096,128]{1,0:T(8,128)(2,1)S(1)}, bf16[4096,128]{1,0:T(8,128)(2,1)S(1)}, u32[]{:S(2)}, u32[]{:S(2)}) %collective-permute-start.1) | collective-permute-done | bytes 1048608 | tf_op jit(solution)/shard_map/ppermute | solution.py:388
  31.1 0.0 copy-start.2
  31.1 0.0 copy-start.5
  31.1 0.0 copy-start.6
  31.1 8.9 %shard_map.89 = (bf16[4096,128]{1,0:T(8,128)(2,1)S(1)}, bf16[4096,128]{1,0:T(8,128)(2,1)S(1)}) custom-call(s32[8192]{0:T(1024)S(1)} %get-tuple-element.9.row_index, s32[8192]{0:T(1024)S(1)} %get-tuple-element.10.col_index, s32[1]{0:T(128)S(6)} %copy.10.count, s32[1]{0:T(128)} %bitcast.place.which, bf16[8192,512]{1,0:T(8,128)(2,1)} %weights.1, ...), custom_call_target="tpu_custom_call" | custom-call | tf_op jit(solution)/shard_map/pallas_call | solution.py:183
  40.0 0.1 collective-permute-start.2
  40.1 2.6 %collective-permute-done.2.got = bf16[4096,128]{1,0:T(8,128)(2,1)S(1)} collective-permute-done((bf16[4096,128]{1,0:T(8,128)(2,1)S(1)}, bf16[4096,128]{1,0:T(8,128)(2,1)S(1)}, u32[]{:S(2)}, u32[]{:S(2)}) %collective-permute-start.2) | collective-permute-done | bytes 1048608 | tf_op jit(solution)/shard_map/ppermute | solution.py:392
  42.8 1.5 %shard_map.90 = bf16[4096,128]{1,0:T(8,128)(2,1)} custom-call(bf16[4096,128]{1,0:T(8,128)(2,1)S(1)} %get-tuple-element.12.keep, bf16[4096,128]{1,0:T(8,128)(2,1)S(1)} %collective-permute-done.2.got), custom_call_target="tpu_custom_call" | custom-call | tf_op jit(solution)/shard_map/pallas_call | solution.py:200
  44.3 8.8 %all-to-all-start.1 = ((bf16[8,512,128]{2,1,0:T(8,128)(2,1)}), bf16[8,512,128]{2,1,0:T(8,128)(2,1)S(1)}, u32[]{:S(2)}, u32[]{:S(2)}) async-start(bf16[8,512,128]{2,1,0:T(8,128)(2,1)} %bitcast.4), calls=%async_computation.1 | async-start | bytes 2097152 | tf_op jit(solution)/shard_map/all_to_all | solution.py:394
  53.1 10.6 %all-to-all-done.1.parts = bf16[8,512,128]{2,1,0:T(8,128)(2,1)S(1)} async-done(((bf16[8,512,128]{2,1,0:T(8,128)(2,1)}), bf16[8,512,128]{2,1,0:T(8,128)(2,1)S(1)}, u32[]{:S(2)}, u32[]{:S(2)}) %all-to-all-start.1) | async-done | bytes 1048608 | tf_op jit(solution)/shard_map/all_to_all | solution.py:394
  63.7 0.1 shard_map.92
  63.9 3.7 %collective-permute-start.3 = (bf16[256,128]{1,0:T(8,128)(2,1)S(1)}, bf16[256,128]{1,0:T(8,128)(2,1)S(1)}, u32[]{:S(2)}, u32[]{:S(2)}) collective-permute-start(bf16[256,128]{1,0:T(8,128)(2,1)S(1)} %shard_map.92), channel_id=1, source_target_pairs={{0,1},{1,0},{2,3},{3,2},{4,5},{5,4},{6,7},{7,6},{8,9},{9,8},{10,11... | collective-permute-start | bytes 196616 | tf_op jit(solution)/shard_map/ppermute | solution.py:402
  67.6 0.1 shard_map.91.here
  67.7 0.8 collective-permute-done.3.there
  68.5 0.0 copy-done.2
  68.5 0.0 copy-done.5
  68.5 0.0 copy-done.6
  68.5 0.0 copy-start.1
  68.5 2.2 %copy-done.1 = bf16[64,64,512]{2,1,0:T(8,128)(2,1)S(1)} copy-done((bf16[64,64,512]{2,1,0:T(8,128)(2,1)S(1)}, bf16[64,64,512]{2,1,0:T(8,128)(2,1)}, u32[]{:S(2)}) %copy-start.1) | copy-done | bytes 4194328
  70.7 1.3 %shard_map.93 = (f32[4096]{0:T(1024)S(1)}, f32[128,128]{1,0:T(8,128)S(1)}) custom-call(f32[256,128]{1,0:T(8,128)S(1)} %shard_map.91.here, bf16[256,128]{1,0:T(8,128)(2,1)S(1)} %collective-permute-done.3.there, bf16[4096,512]{1,0:T(8,128)(2,1)S(1)} %bitcast.11, f32[4096]{0:T(1024)S(1)} %copy-done.5, f32[4096]{0:T(1024)S(1)} %copy-done.6, f32[20,4096]{1,0:T(8,128)S(1)} %copy-done.2), custom_call_target="tpu_custom_call" | custom-call | tf_op jit(solution)/shard_map/pallas_call | solution.py:326
  72.0 18.8 %all_to_all.22 = f32[128,1,128]{2,1,0:T(1,128)S(1)} all-to-all(f32[128,1,128]{2,1,0:T(1,128)S(1)} %bitcast.15), channel_id=1, replica_groups=mesh['zl'=2,'x'=4,'zh'=2,'y'=4,'c'=2] {'zl','x','zh','y','c'}, dimensions={0} | all-to-all | bytes 131072 | tf_op jit(solution)/shard_map/all_to_all | solution.py:403
  90.8 0.8 shard_map.94
  (1 shorter events, 0.0 us)
Async XLA Ops:
  0.6 2.2 %copy-start = (bf16[64,64,512]{2,1,0:T(8,128)(2,1)S(1)}, bf16[64,64,512]{2,1,0:T(8,128)(2,1)}, u32[]{:S(2)}) copy-start(bf16[64,64,512]{2,1,0:T(8,128)(2,1)} %param.9) | copy-start | bytes 12582916
  0.6 0.9 copy-start.4
  1.5 4.3 %copy-start.3 = (s32[2,8192]{1,0:T(2,128)S(1)}, s32[2,8192]{1,0:T(2,128)}, u32[]{:S(2)}) copy-start(s32[2,8192]{1,0:T(2,128)} %pair_index.1) | copy-start | bytes 196612
  3.5 2.3 %collective-permute-start = (bf16[256,128]{1,0:T(8,128)(2,1)S(1)}, bf16[256,128]{1,0:T(8,128)(2,1)S(1)}, u32[]{:S(2)}, u32[]{:S(2)}) collective-permute-start(bf16[256,128]{1,0:T(8,128)(2,1)S(1)} %shard_map.87.local), channel_id=1, source_target_pairs={{0,1},{1,0},{2,3},{3,2},{4,5},{5,4},{6,7},{7,6},{8,9},{9,8},{10,11... | collective-permute-start | bytes 196616 | tf_op jit(solution)/shard_map/ppermute | solution.py:380
  23.3 7.8 %collective-permute-start.1 = (bf16[4096,128]{1,0:T(8,128)(2,1)S(1)}, bf16[4096,128]{1,0:T(8,128)(2,1)S(1)}, u32[]{:S(2)}, u32[]{:S(2)}) collective-permute-start(bf16[4096,128]{1,0:T(8,128)(2,1)S(1)} %bitcast.12), channel_id=1, source_target_pairs={{0,1},{1,0},{2,3},{3,2},{4,5},{5,4},{6,7},{7,6},{8,9},{9,8},{10,11... | collective-permute-start | bytes 3145736 | tf_op jit(solution)/shard_map/ppermute | solution.py:388
  31.1 37.3 %copy-start.2 = (f32[20,4096]{1,0:T(8,128)S(1)}, f32[20,4096]{1,0:T(8,128)}, u32[]{:S(2)}) copy-start(f32[20,4096]{1,0:T(8,128)} %recycled.3) | copy-start | bytes 983044
  31.1 37.3 %copy-start.5 = (f32[4096]{0:T(1024)S(1)}, f32[4096]{0:T(1024)}, u32[]{:S(2)}) copy-start(f32[4096]{0:T(1024)} %trial.3) | copy-start | bytes 49156
  31.1 37.3 %copy-start.6 = (f32[4096]{0:T(1024)S(1)}, f32[4096]{0:T(1024)}, u32[]{:S(2)}) copy-start(f32[4096]{0:T(1024)} %energies.1) | copy-start | bytes 49156
  40.0 2.7 %collective-permute-start.2 = (bf16[4096,128]{1,0:T(8,128)(2,1)S(1)}, bf16[4096,128]{1,0:T(8,128)(2,1)S(1)}, u32[]{:S(2)}, u32[]{:S(2)}) collective-permute-start(bf16[4096,128]{1,0:T(8,128)(2,1)S(1)} %get-tuple-element.13), channel_id=1, source_target_pairs={{0,1},{1,0},{2,3},{3,2},{4,5},{5,4},{6,7},{7,6},{8,9},{9,8},{10,11... | collective-permute-start | bytes 3145736 | tf_op jit(solution)/shard_map/ppermute | solution.py:392
  44.3 19.4 %all-to-all-start.1 = ((bf16[8,512,128]{2,1,0:T(8,128)(2,1)}), bf16[8,512,128]{2,1,0:T(8,128)(2,1)S(1)}, u32[]{:S(2)}, u32[]{:S(2)}) async-start(bf16[8,512,128]{2,1,0:T(8,128)(2,1)} %bitcast.4), calls=%async_computation.1 | async-start | bytes 2097152 | tf_op jit(solution)/shard_map/all_to_all | solution.py:394
  63.9 4.6 %collective-permute-start.3 = (bf16[256,128]{1,0:T(8,128)(2,1)S(1)}, bf16[256,128]{1,0:T(8,128)(2,1)S(1)}, u32[]{:S(2)}, u32[]{:S(2)}) collective-permute-start(bf16[256,128]{1,0:T(8,128)(2,1)S(1)} %shard_map.92), channel_id=1, source_target_pairs={{0,1},{1,0},{2,3},{3,2},{4,5},{5,4},{6,7},{7,6},{8,9},{9,8},{10,11... | collective-permute-start | bytes 196616 | tf_op jit(solution)/shard_map/ppermute | solution.py:402
  68.5 2.2 %copy-start.1 = (bf16[64,64,512]{2,1,0:T(8,128)(2,1)S(1)}, bf16[64,64,512]{2,1,0:T(8,128)(2,1)}, u32[]{:S(2)}) copy-start(bf16[64,64,512]{2,1,0:T(8,128)(2,1)} %param.9) | copy-start | bytes 12582916

commit v2 on v1

--- a/solution.py
+++ b/solution.py
@@ -237,11 +237,12 @@
     lax.fori_loop(0, keep.shape[0] // 16, step, 0, unroll=8)
 
 
-def sum_kernel(which, parts, out):
+def sum_kernel(other, place, parts, out):
     size = out.shape[0]
+    which = 1 - place[0] if other else place[0]
 
     def step(i, _):
-        first = pl.ds(pl.multiple_of(which[0] * size + i * 16, 16), 16)
+        first = pl.ds(pl.multiple_of(which * size + i * 16, 16), 16)
         total = parts[0, first, :].astype(F32)
         for n in range(1, parts.shape[0]):
             total = total + parts[n, first, :].astype(F32)
@@ -394,9 +395,10 @@
     parts = lax.all_to_all(
         total.reshape(row_chips, -1, lanes), AXES, 0, 0, axis_index_groups=groups)
     part = (kpoints * per_k, lanes)
-    away = (1 - core).reshape(1).astype(jnp.int32)
-    there = local_call(sum_kernel, jax.ShapeDtypeStruct(part, BF16), away, parts, scalars=1)
-    here = local_call(sum_kernel, jax.ShapeDtypeStruct(part, F32), place, parts, scalars=1)
+    there = local_call(
+        functools.partial(sum_kernel, True), jax.ShapeDtypeStruct(part, BF16), place, parts, scalars=1)
+    here = local_call(
+        functools.partial(sum_kernel, False), jax.ShapeDtypeStruct(part, F32), place, parts, scalars=1)
     devices = row_chips * col_devices
     product, projections = expand(
         here, lax.ppermute(there, "c", swap), densities, trial, energies, recycled, devices)

time: 91.7 us -> 87.7 us (0.956)
  blocking collectives: 36 us -> 56.3 us
  starting transfers between devices: 19.6 us -> 7.17 us
  waiting for transfers between devices: 16.6 us -> 6.31 us
  local copies, waits for them, and re-layouts: 4.36 us -> 2.18 us
    all_to_all x0 -> x1, blocking collectives: none -> 22.8 us  [body(): lax.all_to_all(total.reshape(row_chips, -1, lanes), AXES, 0, 0, axis_inde...]
    all_to_all x1 -> x0, waiting for transfers between devices: 10.6 us -> none  [body(): lax.all_to_all(total.reshape(row_chips, -1, lanes), AXES, 0, 0, axis_inde...]
    all_to_all x1 -> x0, starting transfers between devices: 8.78 us -> none  [body(): lax.all_to_all(total.reshape(row_chips, -1, lanes), AXES, 0, 0, axis_inde...]
    ppermute x1, starting transfers between devices: 3.69 us -> 0.09 us  [body(): lax.ppermute(there, 'c', swap)]
    all_to_all x1, blocking collectives: 18.8 us -> 16.3 us  [body(): arrived = lax.all_to_all(projections, AXES, 0, 0, tiled=True)]
    unnamed x14, local copies, waits for them, and re-layouts: 4.36 us -> 2.18 us
    pallas_call x5, Pallas kernels: 2.04 us -> 1.04 us  [local_call(): pl.pallas_call(kernel, out_shape=outs, in_specs=[smem] * scalars + [vmem]...]
  transfers between devices with their start and end apart: 5 -> 4, of which waited for: 5 -> 4; matrix products, arithmetic and copies ran while one was open for 0% -> 0% of each run, Pallas kernels for 0% -> 0%
where the time goes in v2:
time: 87.7 us; the launch traced here: 86.9 us
  blocking collectives  56.3 us (64%)
  Pallas kernels  13.6 us (16%)
  starting transfers between devices  7.17 us (8%)
  waiting for transfers between devices  6.31 us (7%)
  local copies, waits for them, and re-layouts  2.18 us (2%)
  between operations  1.39 us (2%)
    all_to_all x1, blocking collectives, body(): lax.all_to_all(total.reshape(row_chips, -1, lanes), AXES, 0, 0, axis_inde...  22.8 us
    all_to_all x1, blocking collectives, body(): lax.all_to_all(spread, AXES, 0, 0, axis_index_groups=groups)  17.2 us
    all_to_all x1, blocking collectives, body(): arrived = lax.all_to_all(projections, AXES, 0, 0, tiled=True)  16.3 us
    pallas_call x1, Pallas kernels, pair_terms(): pl.pallas_call(slot_kernel, out_shape=[jax.ShapeDtypeStruct(mine.shape, B...  9.76 us
    ppermute x1, starting transfers between devices, body(): theirs = lax.ppermute(mine, 'c', swap)  5.56 us
    ppermute x1, waiting for transfers between devices, body(): got = lax.ppermute(send, 'c', swap)  2.65 us
    unnamed x14, local copies, waits for them, and re-layouts  2.18 us
  transfers between devices with their start and end apart: 4, of which 4 were waited for; matrix products, arithmetic and copies ran while one was open for 0% of the time, Pallas kernels for 0%

profile of v2, /device:TPU:1, one launch (start us, length us, event | category | flops | bytes accessed | tf_op | source)
XLA Modules:
  0.0 86.9 jit_solution(18400419213785745000)
XLA Ops:
  0.6 0.0 copy-start
  0.6 0.0 copy-start.4
  0.7 0.9 copy-done.4
  1.5 0.0 copy-start.3
  1.5 1.3 %copy-done = bf16[64,64,512]{2,1,0:T(8,128)(2,1)S(1)} copy-done((bf16[64,64,512]{2,1,0:T(8,128)(2,1)S(1)}, bf16[64,64,512]{2,1,0:T(8,128)(2,1)}, u32[]{:S(2)}) %copy-start) | copy-done | bytes 4194328
  2.8 0.7 shard_map.87.local
  3.5 1.4 %collective-permute-start = (bf16[256,128]{1,0:T(8,128)(2,1)S(1)}, bf16[256,128]{1,0:T(8,128)(2,1)S(1)}, u32[]{:S(2)}, u32[]{:S(2)}) collective-permute-start(bf16[256,128]{1,0:T(8,128)(2,1)S(1)} %shard_map.87.local), channel_id=1, source_target_pairs={{0,1},{1,0},{2,3},{3,2},{4,5},{5,4},{6,7},{7,6},{8,9},{9,8},{10,11... | collective-permute-start | bytes 196616 | tf_op jit(solution)/shard_map/ppermute | solution.py:381
  4.9 0.9 %collective-permute-done.other = bf16[256,128]{1,0:T(8,128)(2,1)S(1)} collective-permute-done((bf16[256,128]{1,0:T(8,128)(2,1)S(1)}, bf16[256,128]{1,0:T(8,128)(2,1)S(1)}, u32[]{:S(2)}, u32[]{:S(2)}) %collective-permute-start) | collective-permute-done | bytes 65568 | tf_op jit(solution)/shard_map/ppermute | solution.py:381
  5.8 0.0 copy-done.3
  5.8 0.3 shard_map.88
  6.1 17.2 %all_to_all.21 = bf16[8,512,128]{2,1,0:T(8,128)(2,1)S(1)} all-to-all(bf16[8,512,128]{2,1,0:T(8,128)(2,1)S(1)} %get-tuple-element.11), channel_id=1, replica_groups={{0,2,4,6,8,10,12,14},{16,18,20,22,24,26,28,30},{32,34,36,38,40,42,44,46..., dimensions={0} | all-to-all | bytes 2097152 | tf_op jit(solution)/shard_map/all_to_all | solution.py:388
  23.3 5.6 %collective-permute-start.1 = (bf16[4096,128]{1,0:T(8,128)(2,1)S(1)}, bf16[4096,128]{1,0:T(8,128)(2,1)S(1)}, u32[]{:S(2)}, u32[]{:S(2)}) collective-permute-start(bf16[4096,128]{1,0:T(8,128)(2,1)S(1)} %bitcast.12), channel_id=1, source_target_pairs={{0,1},{1,0},{2,3},{3,2},{4,5},{5,4},{6,7},{7,6},{8,9},{9,8},{10,11... | collective-permute-start | bytes 3145736 | tf_op jit(solution)/shard_map/ppermute | solution.py:389
  29.5 1.6 %collective-permute-done.1.theirs = bf16[4096,128]{1,0:T(8,128)(2,1)S(1)} collective-permute-done((bf16[4096,128]{1,0:T(8,128)(2,1)S(1)}, bf16[4096,128]{1,0:T(8,128)(2,1)S(1)}, u32[]{:S(2)}, u32[]{:S(2)}) %collective-permute-start.1) | collective-permute-done | bytes 1048608 | tf_op jit(solution)/shard_map/ppermute | solution.py:389
  31.1 0.0 copy-start.1
  31.1 0.0 copy-start.2
  31.1 0.0 copy-start.5
  31.1 0.0 copy-start.6
  31.1 9.8 %shard_map.89 = (bf16[4096,128]{1,0:T(8,128)(2,1)S(1)}, bf16[4096,128]{1,0:T(8,128)(2,1)S(1)}) custom-call(s32[8192]{0:T(1024)S(1)} %get-tuple-element.9.row_index, s32[8192]{0:T(1024)S(1)} %get-tuple-element.10.col_index, s32[1]{0:T(128)S(6)} %copy.10.count, s32[1]{0:T(128)} %bitcast.place, bf16[8192,512]{1,0:T(8,128)(2,1)} %weights.1, ...), custom_call_target="tpu_custom_call" | custom-call | tf_op jit(solution)/shard_map/pallas_call | solution.py:183
  40.9 0.1 collective-permute-start.2
  41.0 2.6 %collective-permute-done.2.got = bf16[4096,128]{1,0:T(8,128)(2,1)S(1)} collective-permute-done((bf16[4096,128]{1,0:T(8,128)(2,1)S(1)}, bf16[4096,128]{1,0:T(8,128)(2,1)S(1)}, u32[]{:S(2)}, u32[]{:S(2)}) %collective-permute-start.2) | collective-permute-done | bytes 1048608 | tf_op jit(solution)/shard_map/ppermute | solution.py:393
  43.7 0.5 shard_map.90
  44.2 22.8 %all_to_all.22.parts = bf16[8,512,128]{2,1,0:T(8,128)(2,1)S(1)} all-to-all(bf16[8,512,128]{2,1,0:T(8,128)(2,1)S(1)} %bitcast.9), channel_id=1, replica_groups={{0,2,4,6,8,10,12,14},{16,18,20,22,24,26,28,30},{32,34,36,38,40,42,44,46..., dimensions={0} | all-to-all | bytes 2097152 | tf_op jit(solution)/shard_map/all_to_all | solution.py:395
  67.0 0.1 shard_map.92
  67.1 0.1 collective-permute-start.3
  67.2 0.1 shard_map.91.here
  67.3 1.1 %collective-permute-done.3.there = bf16[256,128]{1,0:T(8,128)(2,1)S(1)} collective-permute-done((bf16[256,128]{1,0:T(8,128)(2,1)S(1)}, bf16[256,128]{1,0:T(8,128)(2,1)S(1)}, u32[]{:S(2)}, u32[]{:S(2)}) %collective-permute-start.3) | collective-permute-done | bytes 65568 | tf_op jit(solution)/shard_map/ppermute | solution.py:404
  68.4 0.0 copy-done.1
  68.4 0.0 copy-done.2
  68.4 0.0 copy-done.5
  68.5 0.0 copy-done.6
  68.5 1.3 %shard_map.93 = (f32[4096]{0:T(1024)S(1)}, f32[128,128]{1,0:T(8,128)S(1)}) custom-call(f32[256,128]{1,0:T(8,128)S(1)} %shard_map.91.here, bf16[256,128]{1,0:T(8,128)(2,1)S(1)} %collective-permute-done.3.there, bf16[4096,512]{1,0:T(8,128)(2,1)S(1)} %bitcast.11, f32[4096]{0:T(1024)S(1)} %copy-done.5, f32[4096]{0:T(1024)S(1)} %copy-done.6, f32[20,4096]{1,0:T(8,128)S(1)} %copy-done.2), custom_call_target="tpu_custom_call" | custom-call | tf_op jit(solution)/shard_map/pallas_call | solution.py:327
  69.8 16.3 %all_to_all.23 = f32[128,1,128]{2,1,0:T(1,128)S(1)} all-to-all(f32[128,1,128]{2,1,0:T(1,128)S(1)} %bitcast.15), channel_id=1, replica_groups=mesh['zl'=2,'x'=4,'zh'=2,'y'=4,'c'=2] {'zl','x','zh','y','c'}, dimensions={0} | all-to-all | bytes 131072 | tf_op jit(solution)/shard_map/all_to_all | solution.py:405
  86.1 0.8 shard_map.94
  (1 shorter events, 0.0 us)
Async XLA Ops:
  0.6 2.2 %copy-start = (bf16[64,64,512]{2,1,0:T(8,128)(2,1)S(1)}, bf16[64,64,512]{2,1,0:T(8,128)(2,1)}, u32[]{:S(2)}) copy-start(bf16[64,64,512]{2,1,0:T(8,128)(2,1)} %param.9) | copy-start | bytes 12582916
  0.6 0.9 %copy-start.4 = (f32[4096]{0:T(1024)S(1)}, f32[4096]{0:T(1024)}, u32[]{:S(2)}) copy-start(f32[4096]{0:T(1024)} %trial.3) | copy-start | bytes 49156
  1.5 4.3 %copy-start.3 = (s32[2,8192]{1,0:T(2,128)S(1)}, s32[2,8192]{1,0:T(2,128)}, u32[]{:S(2)}) copy-start(s32[2,8192]{1,0:T(2,128)} %pair_index.1) | copy-start | bytes 196612
  3.5 2.3 %collective-permute-start = (bf16[256,128]{1,0:T(8,128)(2,1)S(1)}, bf16[256,128]{1,0:T(8,128)(2,1)S(1)}, u32[]{:S(2)}, u32[]{:S(2)}) collective-permute-start(bf16[256,128]{1,0:T(8,128)(2,1)S(1)} %shard_map.87.local), channel_id=1, source_target_pairs={{0,1},{1,0},{2,3},{3,2},{4,5},{5,4},{6,7},{7,6},{8,9},{9,8},{10,11... | collective-permute-start | bytes 196616 | tf_op jit(solution)/shard_map/ppermute | solution.py:381
  23.3 7.8 %collective-permute-start.1 = (bf16[4096,128]{1,0:T(8,128)(2,1)S(1)}, bf16[4096,128]{1,0:T(8,128)(2,1)S(1)}, u32[]{:S(2)}, u32[]{:S(2)}) collective-permute-start(bf16[4096,128]{1,0:T(8,128)(2,1)S(1)} %bitcast.12), channel_id=1, source_target_pairs={{0,1},{1,0},{2,3},{3,2},{4,5},{5,4},{6,7},{7,6},{8,9},{9,8},{10,11... | collective-permute-start | bytes 3145736 | tf_op jit(solution)/shard_map/ppermute | solution.py:389
  31.1 37.3 %copy-start.1 = (bf16[64,64,512]{2,1,0:T(8,128)(2,1)S(1)}, bf16[64,64,512]{2,1,0:T(8,128)(2,1)}, u32[]{:S(2)}) copy-start(bf16[64,64,512]{2,1,0:T(8,128)(2,1)} %param.9) | copy-start | bytes 12582916
  31.1 37.3 %copy-start.2 = (f32[20,4096]{1,0:T(8,128)S(1)}, f32[20,4096]{1,0:T(8,128)}, u32[]{:S(2)}) copy-start(f32[20,4096]{1,0:T(8,128)} %recycled.3) | copy-start | bytes 983044
  31.1 37.3 %copy-start.5 = (f32[4096]{0:T(1024)S(1)}, f32[4096]{0:T(1024)}, u32[]{:S(2)}) copy-start(f32[4096]{0:T(1024)} %trial.3) | copy-start | bytes 49156
  31.1 37.3 %copy-start.6 = (f32[4096]{0:T(1024)S(1)}, f32[4096]{0:T(1024)}, u32[]{:S(2)}) copy-start(f32[4096]{0:T(1024)} %energies.1) | copy-start | bytes 49156
  40.9 2.7 %collective-permute-start.2 = (bf16[4096,128]{1,0:T(8,128)(2,1)S(1)}, bf16[4096,128]{1,0:T(8,128)(2,1)S(1)}, u32[]{:S(2)}, u32[]{:S(2)}) collective-permute-start(bf16[4096,128]{1,0:T(8,128)(2,1)S(1)} %get-tuple-element.13), channel_id=1, source_target_pairs={{0,1},{1,0},{2,3},{3,2},{4,5},{5,4},{6,7},{7,6},{8,9},{9,8},{10,11... | collective-permute-start | bytes 3145736 | tf_op jit(solution)/shard_map/ppermute | solution.py:393
  67.1 1.3 %collective-permute-start.3 = (bf16[256,128]{1,0:T(8,128)(2,1)S(1)}, bf16[256,128]{1,0:T(8,128)(2,1)S(1)}, u32[]{:S(2)}, u32[]{:S(2)}) collective-permute-start(bf16[256,128]{1,0:T(8,128)(2,1)S(1)} %shard_map.92), channel_id=1, source_target_pairs={{0,1},{1,0},{2,3},{3,2},{4,5},{5,4},{6,7},{7,6},{8,9},{9,8},{10,11... | collective-permute-start | bytes 196616 | tf_op jit(solution)/shard_map/ppermute | solution.py:404
